TPU v7x, 256 devices: a whole 4x4x8 slice. The times are simulated.
256 devices in a mesh: context: 64 (over z, y, core), dp: 4 (over x).
Axes of the slice: x: 4, y: 4, z: 8, core: 2. Of those that a mesh axis runs over, the one named last changes fastest.
Arguments:
- tokens: bfloat16 [4, 16384, 8192], P('dp', 'context'), may hold values from -16 to 16
- projection: bfloat16 [8192, 1280], P(('context', 'dp')), may hold values from -0.09375 to 0.09375
- doc_lengths: int32 [4, 6], P('dp'), may hold values from 1 to 8192, 16384 in all within a row
Outputs:
- attended: bfloat16 [4, 16384, 1024], P('dp', 'context')
Inputs may be any that keep to these rules, and one draw needn't show every extreme that they name: `doc_lengths`: each row's lengths sum to 16384, and some document has exactly 8192 tokens.
All inputs are finite; a program needn't handle non-finite values.
Results may differ from a plain program's by a relative error of at most 0.007.
The roundings to bfloat16 on the way count: a program that leaves them out, or rounds other values in their place, can miss the bound.
Values may be sent and summed in bfloat16 or wider, within the bound.
No kernel may reach another device: no remote copies, remote signals or barrier semaphores. Data moves between devices by JAX's collectives and lax.ppermute only.
A program may use at most 64 MiB of HBM per device.

v0:
```python
import jax
import jax.numpy as jnp
from jax import lax
from jax.sharding import PartitionSpec as P

HEADS = 8
HEAD = 128


def doc_tables(lengths, tpos):
    ends = jnp.cumsum(lengths)
    after = tpos[:, None] >= ends[None, :]
    docid = jnp.sum(after.astype(jnp.int32), axis=1)
    begin = jnp.sum(jnp.where(after, lengths[None, :], 0), axis=1)
    return (docid, begin)


def rotate(vecs, pos):
    half = vecs.shape[-1] // 2
    expo = jnp.arange(half).astype(jnp.float32) * (2.0 / vecs.shape[-1])
    inv = jnp.power(jnp.float32(500000.0), -expo)
    angle = pos[:, None] * inv[None, :]
    cosine = jnp.cos(angle)[:, None, :]
    sine = jnp.sin(angle)[:, None, :]
    first = vecs[..., :half]
    second = vecs[..., half:]
    return jnp.concatenate(
        [first * cosine - second * sine, second * cosine + first * sine], axis=-1
    )


def per_device(tokens, projection, doc_lengths):
    tok = tokens.shape[1]
    rows = tokens[0]
    lengths = doc_lengths[0]
    span = HEADS * HEAD
    here = lax.axis_index("context")
    proj = jnp.dot(
        rows,
        lax.all_gather(projection, ("context", "dp"), axis=0, tiled=True),
        preferred_element_type=jnp.float32,
    )
    qtok = here * tok + jnp.arange(tok, dtype=jnp.int32)
    qdoc, qbegin = doc_tables(lengths, qtok)
    pos = (qtok - qbegin).astype(jnp.float32)
    queries = rotate(proj[:, :span].reshape(tok, HEADS, HEAD), pos).astype(jnp.bfloat16)
    keys = (
        rotate(proj[:, span : span + HEAD].reshape(tok, 1, HEAD), pos)
        .reshape(tok, HEAD)
        .astype(jnp.bfloat16)
    )
    values = proj[:, span + HEAD :].astype(jnp.bfloat16)
    keyval = jnp.concatenate([keys, values], axis=1)
    scale = HEAD ** (-0.5)

    def visit(carry, block, kstart):
        ktok = kstart + jnp.arange(block.shape[0], dtype=jnp.int32)
        kdoc, kbegin = doc_tables(lengths, ktok)
        visible = (
            (kdoc[None, :] == qdoc[:, None])
            & (ktok[None, :] <= qtok[:, None])
            & (ktok[None, :] >= 0)
        )

        def compute(state):
            top, total, accum = state
            scores = (
                jnp.einsum(
                    "qhd,kd->hqk", queries, block[:, :HEAD], preferred_element_type=jnp.float32
                )
                * scale
            )
            scores = jnp.where(visible[None], scores, -1e30)
            newtop = jnp.maximum(top, jnp.max(scores, axis=-1))
            factor = jnp.exp(top - newtop)
            weights = jnp.exp(scores - newtop[..., None]) * visible[None].astype(jnp.float32)
            total = total * factor + jnp.sum(weights, axis=-1)
            accum = accum * factor[..., None] + jnp.einsum(
                "hqk,kd->hqd", weights, block[:, HEAD:].astype(jnp.float32)
            )
            return (newtop, total, accum)

        return lax.cond(jnp.any(visible), compute, lambda state: state, carry)

    init = (
        jnp.full((HEADS, tok), -1e30, jnp.float32),
        jnp.zeros((HEADS, tok), jnp.float32),
        jnp.zeros((HEADS, tok, HEAD), jnp.float32),
    )
    carry = init
    piece = lax.all_gather(keyval, "context", axis=0, tiled=True)
    count = piece.shape[0] // tok
    pieces = piece.reshape(count, tok, 2 * HEAD)
    starts = jnp.arange(count, dtype=jnp.int32) * tok

    def one_block(state, item):
        return (visit(state, item[0], item[1]), None)

    carry, unused = lax.scan(one_block, carry, (pieces, starts))
    top, total, accum = carry
    mixed = accum / total[..., None]
    return jnp.transpose(mixed, (1, 0, 2)).reshape(1, tok, span).astype(jnp.bfloat16)


def solution(mesh):
    in_specs = (P("dp", "context", None), P(("context", "dp"), None), P("dp", None))
    out_specs = P("dp", "context", None)
    return jax.shard_map(
        per_device, mesh=mesh, in_specs=in_specs, out_specs=out_specs, check_vma=False
    )
```

profile of v0, /device:TPU:244, one launch (start us, length us, event | category | flops | bytes accessed | tf_op | source)
XLA Modules:
  0.0 564.1 jit_solution(10544613095609087572)
XLA Ops:
  8.9 129.8 %all-gather.3.cloned.1.call-done = bf16[8192,1280]{1,0:T(8,128)(2,1)} async-done(((bf16[32,1280]{1,0:T(8,128)(2,1)}), bf16[8192,1280]{1,0:T(8,128)(2,1)}) %all-gather.3.cloned.1.call-update) | async-done | bytes 20971536 | tf_op jit(solution)/shard_map/all_gather | solution.py:40
  138.7 12.2 %fusion.14 = f32[256,1280]{1,0:T(8,128)S(1)} fusion(bf16[8192,1280]{1,0:T(8,128)(2,1)} %all-gather.3.cloned.1.call-done, bf16[1,256,8192]{2,1,0:T(8,128)(2,1)} %param.7), kind=kOutput, calls=%fused_computation.25 | convolution fusion | flops 5368709120 | bytes 26476544 | tf_op jit(solution)/shard_map/dot_general | solution.py:38
  154.3 84.8 %all-gather.5.cloned.1.call-done = bf16[16384,256]{0,1:T(8,128)(2,1)} async-done(((bf16[256,256]{0,1:T(8,128)(2,1)}), bf16[16384,256]{0,1:T(8,128)(2,1)}) %all-gather.5.cloned.1.call-update) | async-done | bytes 8388624 | tf_op jit(solution)/shard_map/all_gather | solution.py:91
  239.1 11.9 %copy.20 = bf16[16384,256]{1,0:T(8,128)(2,1)} copy(bf16[16384,256]{0,1:T(8,128)(2,1)} %all-gather.5.cloned.1.call-done) | data formatting | bytes 16777216
  251.1 304.4 %while.17 = (s32[]{:T(128)}, f32[8,256]{1,0:T(8,128)S(1)}, f32[8,256]{1,0:T(8,128)S(1)}, f32[8,256,128]{2,1,0:T(8,128)S(1)}, s32[64]{0:T(128)S(1)}, /*index=5*/s...) while((s32[]{:T(128)}, f32[8,256]{1,0:T(8,128)S(1)}, ...), condition=%wide.region_11.12_spmd.clone, body=%wide.region_4.11_spmd.clone.sunk | while | flops 275653888 | bytes 10560287 | solution.py:99
  343.7 3.0 conditional.3
  349.9 3.0 conditional.3
  356.2 3.0 conditional.3
  362.4 3.0 conditional.3
  368.6 3.0 conditional.3
  374.8 3.0 conditional.3
  381.1 3.0 conditional.3
  387.3 3.0 conditional.3
  393.5 3.0 conditional.3
  399.7 3.0 conditional.3
  406.0 3.0 conditional.3
  412.2 3.0 conditional.3
  418.4 3.0 conditional.3
  424.6 3.0 conditional.3
  443.3 3.0 conditional.3
  449.5 3.0 conditional.3
  455.7 3.0 conditional.3
  505.5 3.0 conditional.3
  511.8 3.0 conditional.3
  (661 shorter events, 312.9 us)
Async XLA Ops:
  6.5 132.2 %all-gather.3.cloned.1.call-start = ((), (), s32[]{:S(2)}) async-start(), calls=%async_computation | async-start | bytes 21053440 | tf_op jit(solution)/shard_map/all_gather | solution.py:40
  7.3 231.8 %all-gather.5.cloned.1.call-start = ((), (), s32[]{:S(2)}) async-start(), calls=%async_computation.1 | async-start | bytes 8519680 | tf_op jit(solution)/shard_map/all_gather | solution.py:91
  8.9 143.3 %copy-start = (s32[1,6]{1,0:T(1,128)S(1)}, s32[1,6]{1,0:T(1,128)}, u32[]{:S(2)}) copy-start(s32[1,6]{1,0:T(1,128)} %param.9) | copy-start | bytes 76
Sparse Core Ops, SparseCore 0:
  10.9 127.7 all-gather.2
  152.3 86.7 all-gather.4
where the time goes:
time: 567 us; the launch traced here: 564 us
  waiting for transfers between devices  215 us (38%)
  other arithmetic  151 us (27%)
  local copies, waits for them, and re-layouts  80.5 us (14%)
  matrix products  61.7 us (11%)
  loops' own time  42 us (7%)
  between operations  13.5 us (2%)
    all_gather x1, waiting for transfers between devices, per_device(): lax.all_gather(projection, ('context', 'dp'), axis=0, tiled=True)  130 us
    all_gather x1, waiting for transfers between devices, per_device(): piece = lax.all_gather(keyval, 'context', axis=0, tiled=True)  84.8 us
    reduce_or x64, other arithmetic, visit(): return lax.cond(jnp.any(visible), compute, lambda state: state, carry)  49.9 us
    another operation x1, loops' own time, per_device(): carry, unused = lax.scan(one_block, carry, (pieces, starts))  39.3 us
    ge x64, other arithmetic, visit(): ktok[None, :] >= 0  36.6 us
    add x65, other arithmetic, per_device(): qtok = here * tok + jnp.arange(tok, dtype=jnp.int32)  36.5 us
    dynamic_slice x64, local copies, waits for them, and re-layouts, per_device(): carry, unused = lax.scan(one_block, carry, (pieces, starts))  35.8 us
    dot_general x33, matrix products, compute(): jnp.einsum('hqk,kd->hqd', weights, block[:, HEAD:].astype(jnp.float32))  34 us
  transfers between devices with their start and end apart: 2, of which 2 were waited for; matrix products, arithmetic and copies ran while one was open for 1% of the time, Pallas kernels for 0%

commit v1 on v0

v1 whole, which is shorter than its diff:
```python
import functools

import jax
import jax.numpy as jnp
import numpy as np
from jax import lax
from jax.experimental import pallas as pl
from jax.experimental.pallas import tpu as pltpu
from jax.sharding import PartitionSpec as P

HEADS = 8
HEAD = 128
REACH = 8192
KB = 1024
LOG2E = 1.4426950408889634


def doc_tables(lengths, tpos):
    ends = jnp.cumsum(lengths)
    after = tpos[:, None] >= ends[None, :]
    return jnp.sum(jnp.where(after, lengths[None, :], 0), axis=1).astype(jnp.int32)


def rotate(vecs, pos):
    half = vecs.shape[-1] // 2
    expo = jnp.arange(half).astype(jnp.float32) * (2.0 / vecs.shape[-1])
    inv = jnp.power(jnp.float32(500000.0), -expo)
    angle = pos[:, None] * inv[None, :]
    cosine = jnp.cos(angle)[:, None, :]
    sine = jnp.sin(angle)[:, None, :]
    first = vecs[..., :half]
    second = vecs[..., half:]
    return jnp.concatenate(
        [first * cosine - second * sine, second * cosine + first * sine], axis=-1
    )


def attend_kernel(heads, span_ref, begin_ref, q_ref, kv_hbm, out_ref, kvbuf, top, total, accum, sem):
    start, low, high, full_low, full_high = [span_ref[i] for i in range(5)]
    tok = q_ref.shape[0]
    factor = np.float32(HEAD**-0.5 * LOG2E)

    def fetch(i):
        return pltpu.make_async_copy(
            kv_hbm.at[pl.ds(pl.multiple_of(i * KB, KB), KB)], kvbuf.at[i - low], sem.at[i - low]
        )

    @pl.loop(low, high)
    def _(i):
        fetch(i).start()

    top[...] = jnp.full(top.shape, -1e30, jnp.float32)
    total[...] = jnp.zeros(total.shape, jnp.float32)
    accum[...] = jnp.zeros(accum.shape, jnp.float32)

    def block(i, masked):
        kv = kvbuf[i - low]
        keys = kv[:, :HEAD]
        values = kv[:, HEAD:]
        if masked:
            ktok = lax.broadcasted_iota(jnp.int32, (tok, KB), 1) + i * KB
            qtok = lax.broadcasted_iota(jnp.int32, (tok, KB), 0) + start
            visible = (ktok >= begin_ref[:, 0:1]) & (ktok <= qtok)
        for h in range(heads):
            scores = lax.dot_general(
                q_ref[:, h * HEAD : (h + 1) * HEAD],
                keys,
                (((1,), (1,)), ((), ())),
                preferred_element_type=jnp.float32,
            )
            if masked:
                scores = jnp.where(visible, scores, -1e30)
            old = top[h]
            new = jnp.maximum(old, jnp.max(scores, axis=1, keepdims=True))
            shrink = jnp.exp2((old - new) * factor)
            weights = jnp.exp2((scores - jnp.tile(new, (1, KB // HEAD))) * factor)
            top[h] = new
            total[h] = total[h] * shrink + jnp.sum(weights, axis=1, keepdims=True)
            accum[h] = accum[h] * shrink + jnp.dot(
                weights.astype(jnp.bfloat16), values, preferred_element_type=jnp.float32
            )

    @pl.loop(low, high)
    def _(i):
        fetch(i).wait()
        full = (i >= full_low) & (i < full_high)

        @pl.when(full)
        def _():
            block(i, False)

        @pl.when(jnp.logical_not(full))
        def _():
            block(i, True)

    for h in range(heads):
        out_ref[:, h * HEAD : (h + 1) * HEAD] = (accum[h] / total[h]).astype(jnp.bfloat16)


def attend(queries, keyval, begins, start):
    tok = queries.shape[0]
    heads = queries.shape[1] // HEAD
    slots = REACH // KB + 2
    spans = jnp.stack(
        [
            start,
            begins[0] // KB,
            (start + tok + KB - 1) // KB,
            (begins[-1] + KB - 1) // KB,
            (start + 1) // KB,
        ]
    ).astype(jnp.int32)
    vmem = pl.BlockSpec(memory_space=pltpu.VMEM)
    state = pltpu.VMEM((heads, tok, HEAD), jnp.float32)
    return pl.pallas_call(
        functools.partial(attend_kernel, heads),
        out_shape=jax.ShapeDtypeStruct((tok, heads * HEAD), jnp.bfloat16),
        in_specs=[
            pl.BlockSpec(memory_space=pltpu.SMEM),
            vmem,
            vmem,
            pl.BlockSpec(memory_space=pl.ANY),
        ],
        out_specs=vmem,
        scratch_shapes=[
            pltpu.VMEM((slots, KB, 2 * HEAD), jnp.bfloat16),
            state,
            state,
            state,
            pltpu.SemaphoreType.DMA((slots,)),
        ],
        compiler_params=pltpu.CompilerParams(vmem_limit_bytes=48 * 2**20),
        name="attend",
    )(spans, jnp.broadcast_to(begins[:, None], (tok, HEAD)), queries, keyval)


def per_device(tokens, projection, doc_lengths):
    tok = tokens.shape[1]
    rows = tokens[0]
    lengths = doc_lengths[0]
    span = HEADS * HEAD
    here = lax.axis_index("context")
    proj = jnp.dot(
        rows,
        lax.all_gather(projection, ("context", "dp"), axis=0, tiled=True),
        preferred_element_type=jnp.float32,
    )
    start = (here * tok).astype(jnp.int32)
    qtok = start + jnp.arange(tok, dtype=jnp.int32)
    begins = doc_tables(lengths, qtok)
    pos = (qtok - begins).astype(jnp.float32)
    rotated = rotate(proj[:, : span + HEAD].reshape(tok, HEADS + 1, HEAD), pos)
    rotated = rotated.reshape(tok, span + HEAD).astype(jnp.bfloat16)
    values = proj[:, span + HEAD :].astype(jnp.bfloat16)
    keyval = jnp.concatenate([rotated[:, span:], values], axis=1)
    everyone = lax.all_gather(keyval, "context", axis=0, tiled=True)
    return attend(rotated[:, :span], everyone, begins, start)[None]


def solution(mesh):
    in_specs = (P("dp", "context", None), P(("context", "dp"), None), P("dp", None))
    out_specs = P("dp", "context", None)
    return jax.shard_map(
        per_device, mesh=mesh, in_specs=in_specs, out_specs=out_specs, check_vma=False
    )
```

time: 567 us -> 282 us (0.50)
  the two profiles are of different devices: /device:TPU:244 before, /device:TPU:152 now
where the time goes in v1:
time: 282 us
  waiting for transfers between devices  206 us (73%)
  Pallas kernels  41.8 us (15%)
  between operations  16.8 us (6%)
  matrix products  12.1 us (4%)
    all_gather x1, waiting for transfers between devices, per_device(): lax.all_gather(projection, ('context', 'dp'), axis=0, tiled=True)  132 us
    all_gather x1, waiting for transfers between devices, per_device(): everyone = lax.all_gather(keyval, 'context', axis=0, tiled=True)  74 us
    pallas_call x1, Pallas kernels, attend(): pl.pallas_call(functools.partial(attend_kernel, heads), out_shape=jax.Sha...  41.8 us
    dot_general x1, matrix products, per_device(): jnp.dot(rows, lax.all_gather(projection, ('context', 'dp'), axis=0, tiled...  12.1 us
  transfers between devices with their start and end apart: 2, of which 2 were waited for; matrix products, arithmetic and copies ran while one was open for 1% of the time, Pallas kernels for 0%

profile of v1, /device:TPU:152, one launch (start us, length us, event | category | flops | bytes accessed | tf_op | source)
XLA Modules:
  0.0 281.5 jit_solution(2287715547889356260)
XLA Ops:
  6.5 0.0 all-gather.3.cloned.1.call-start
  6.5 0.7 all-gather.3.cloned.1.call-update
  7.3 0.0 all-gather.5.cloned.1.call-start
  7.3 0.8 reduce-window.8
  8.2 0.7 select_reduce_fusion
  8.9 0.3 multiply_cosine_fusion
  9.2 131.6 %all-gather.3.cloned.1.call-done = bf16[8192,1280]{1,0:T(8,128)(2,1)} async-done(((bf16[32,1280]{1,0:T(8,128)(2,1)}), bf16[8192,1280]{1,0:T(8,128)(2,1)}) %all-gather.3.cloned.1.call-update) | async-done | bytes 20971536 | tf_op jit(solution)/shard_map/all_gather | solution.py:145
  140.8 12.1 %fusion = f32[256,1280]{1,0:T(8,128)S(1)} fusion(bf16[8192,1280]{1,0:T(8,128)(2,1)} %all-gather.3.cloned.1.call-done, bf16[1,256,8192]{2,1,0:T(8,128)(2,1)} %param.3), kind=kOutput, calls=%fused_computation | convolution fusion | flops 5368709120 | bytes 26476544 | tf_op jit(solution)/shard_map/dot_general | solution.py:143
  153.0 0.1 slice.33
  153.1 0.4 copy.7
  153.5 0.2 subtract_convert_fusion
  153.7 0.1 copy.11
  153.8 0.7 pad_maximum_fusion.1
  154.5 0.0 all-gather.5.cloned.1.call-update
  154.5 0.6 fusion.2
  158.4 0.1 stack.23.span_ref
  158.5 0.2 copy.10.q_ref
  158.7 74.0 %all-gather.5.cloned.1.call-done.kv_hbm = bf16[16384,256]{1,0:T(8,128)(2,1)} async-done(((bf16[256,256]{1,0:T(8,128)(2,1)}), bf16[16384,256]{1,0:T(8,128)(2,1)}) %all-gather.5.cloned.1.call-update) | async-done | bytes 8388624 | tf_op jit(solution)/shard_map/all_gather | solution.py:156
  232.7 0.1 broadcast_in_dim.32.begin_ref
  232.8 41.8 %attend.1 = bf16[256,1024]{1,0:T(8,128)(2,1)} custom-call(s32[5]{0:T(128)S(1)} %stack.23.span_ref, s32[256,128]{1,0:T(8,128)S(1)} %broadcast_in_dim.32.begin_ref, bf16[256,1024]{1,0:T(8,128)(2,1)S(1)} %copy.10.q_ref, bf16[16384,256]{1,0:T(8,128)(2,1)} %all-gather.5.cloned.1.call-done.kv_hbm), custom_call_target="tpu_custom_call" | custom-call | tf_op jit(solution)/shard_map/attend/pallas_call | solution.py:115
  (7 shorter events, 0.1 us)
Async XLA Ops:
  6.5 134.3 %all-gather.3.cloned.1.call-start = ((), (), s32[]{:S(2)}) async-start(), calls=%async_computation | async-start | bytes 21053440 | tf_op jit(solution)/shard_map/all_gather | solution.py:145
  7.3 225.5 %all-gather.5.cloned.1.call-start = ((), (), s32[]{:S(2)}) async-start(), calls=%async_computation.1 | async-start | bytes 8519680 | tf_op jit(solution)/shard_map/all_gather | solution.py:156
Sparse Core Ops, SparseCore 0:
  10.9 129.8 all-gather.2
  154.6 78.0 all-gather.4
